TPU v7x, 512 devices: a whole 4x8x8 slice. The times are simulated.
512 devices in a mesh: row: 16 (over z, core), col: 32 (over x, y).
Axes of the slice: x: 4, y: 8, z: 8, core: 2. Of those that a mesh axis runs over, the one named last changes fastest.
Arguments:
- front: float32 [12288, 12288], P('row', 'col'), as said below
- structure: int32 [3, 96], replicated, may hold values from 0 to 1, as said below
- factor_front: float32 [3, 12288, 512], P(None, 'row', 'col'), may hold values from -0.0546875 to 0.0546875
- factor_border: float32 [2, 512, 512], replicated, may hold values from -0.6 to 0.6
- pivot_inverse: float32 [3, 512, 512], P(None, 'row')
Outputs:
- inverse_front: float32 [3, 512, 12288], P(None, 'row', 'col')
- inverse_parent: float32 [2, 512, 512], P(None, 'row')
- inverse_diagonal: float32 [3, 512, 512], P(None, 'row')
Inputs may be any that keep to these rules, and one draw needn't show every extreme that they name: front is exactly symmetric. structure[k, b] = 1 where front block b (rows b * 128 to (b + 1) * 128 - 1) lies in supernode k's structure; every 1 in row k is also a 1 in row k - 1; blocks b < 24 are 1 in every row.
All inputs are finite; a program needn't handle non-finite values.
Results may differ from a plain program's by a relative error of at most 0.0001.
Values sent between devices are 32-bit elements; how exact they have to be, the bound alone decides.
A program may use at most 64 MiB of HBM per device.

v0:
```python
import jax
import jax.numpy as jnp
from jax import lax
from jax.sharding import Mesh
from jax.sharding import PartitionSpec as P

BLK = 128
ROW = ("row_0", "row_1")
HIGH = lax.Precision.HIGHEST


def broadcast_by_axis(x, axes, root):
    x = jnp.where(lax.axis_index(axes) == root, x, jnp.zeros_like(x))
    for axis in axes:
        x = lax.psum(x, axis)
    return x


def split_up(x, dim, length):
    dims = x.shape
    pieces = x.reshape(*dims[:dim], length, dims[dim] // length, *dims[dim + 1 :])
    return jnp.moveaxis(pieces, dim, 0)


def sent_and_summed(x, axis, dim):
    length = lax.axis_size(axis)
    pieces = lax.all_to_all(split_up(x, dim, length), axis, 0, 0, tiled=True)
    return jnp.sum(pieces, axis=0)


def padded_to(lines, length):
    spare = -lines.shape[0] % length
    if not spare:
        return lines
    return jnp.concatenate([lines, jnp.zeros((spare, *lines.shape[1:]), lines.dtype)])


def in_order(pieces, dim):
    pieces = jnp.moveaxis(pieces, 0, dim)
    dims = pieces.shape
    return pieces.reshape(*dims[:dim], dims[dim] * dims[dim + 1], *dims[dim + 2 :])


def from_everyone(x, axis):
    copies = jnp.broadcast_to(x, (lax.axis_size(axis), *x.shape))
    return lax.all_to_all(copies, axis, split_axis=0, concat_axis=0, tiled=True)


def collect(x, axis, dim):
    return in_order(from_everyone(x, axis), dim)


def total_of(x, axes):
    lines = x.reshape(-1, x.shape[-1])
    own = sent_and_summed(padded_to(lines, lax.axis_size(axes)), axes, 0)
    whole = collect(own, axes, 0)
    return whole[: len(lines)].reshape(x.shape)


def matmul(former, latter):
    return jnp.dot(former, latter, precision=HIGH, preferred_element_type=jnp.float32)


def contract_first(former, latter):
    return lax.dot_general(
        former, latter, (((0,), (0,)), ((), ())), precision=HIGH, preferred_element_type=jnp.float32
    )


def block_flags(structure_row, first_row, rows_count):
    position = first_row + jnp.arange(rows_count, dtype=jnp.int32)
    owners = position // BLK
    numbers = jnp.arange(structure_row.shape[0], dtype=jnp.int32)
    matches = (owners[:, None] == numbers[None, :]).astype(jnp.float32)
    return jnp.dot(matches, structure_row.astype(jnp.float32), precision=HIGH)


def body(front, structure, factor_front, factor_border, pivot_inverse):
    row_index = lax.axis_index(ROW)
    col_index = lax.axis_index("col")
    rows_here = front.shape[0]
    cols_here = front.shape[1]
    width_here = pivot_inverse.shape[1]
    supers = structure.shape[0]
    row_first = row_index * rows_here
    col_first = col_index * cols_here
    fetched = lax.all_gather(factor_front, "col", axis=2, tiled=True)
    fronts = []
    parents = []
    diagonals = []
    previous = None
    diag_prev = None
    for section in range(supers):
        gathered = fetched[section]
        row_flags = block_flags(structure[section], row_first, rows_here)
        factor_rows = gathered * row_flags[:, None]
        own_half = lax.dynamic_slice_in_dim(factor_rows, col_index % 2 * cols_here, cols_here, 0)
        factor_cols = broadcast_by_axis(own_half, ROW, col_index // 2)
        partial_value = contract_first(factor_rows, front)
        if section > 0:
            border = factor_border[section - 1]
            border_rows = lax.dynamic_slice_in_dim(border, row_index * width_here, width_here, 0)
            partial_value = partial_value + contract_first(border_rows, previous)
            parent_part = total_of(matmul(previous, factor_cols), "col")
            parent_rows = parent_part + matmul(diag_prev, border)
            parent_all = lax.all_gather(parent_rows, ROW, axis=0, tiled=True)
            parents.append(-parent_rows)
        image_rows = sent_and_summed(partial_value, ROW, 0)
        col_flags = block_flags(structure[section], col_first, cols_here)
        current = -(image_rows * col_flags[None, :])
        gram_rows = total_of(matmul(image_rows, factor_cols), "col")
        diag_now = pivot_inverse[section] + gram_rows
        if section > 0:
            parent_slice = lax.dynamic_slice_in_dim(
                parent_all, row_index * width_here, width_here, 1
            )
            diag_now = diag_now + contract_first(parent_slice, border)
        fronts.append(current)
        diagonals.append(diag_now)
        previous = current
        diag_prev = diag_now
    return (jnp.stack(fronts), jnp.stack(parents), jnp.stack(diagonals))


def solution(mesh):
    torus = Mesh(mesh.devices.reshape(8, 2, mesh.shape["col"]), ("row_0", "row_1", "col"))
    return jax.shard_map(
        body,
        mesh=torus,
        in_specs=(P(ROW, "col"), P(), P(None, ROW, "col"), P(), P(None, ROW, None)),
        out_specs=(P(None, ROW, "col"), P(None, ROW, None), P(None, ROW, None)),
        check_vma=False,
    )
```

profile of v0, /device:TPU:1, one launch (start us, length us, event | category | flops | bytes accessed | tf_op | source)
XLA Modules:
  0.0 465.4 jit_solution(13938320989205049159)
XLA Ops:
  11.3 91.5 %all-gather.4.cloned.1.call-done = f32[3,768,512]{1,2,0:T(8,128)} async-done(((f32[3,768,16]{1,2,0:T(8,128)}), f32[3,768,512]{1,2,0:T(8,128)}) %all-gather.4.cloned.1.call-update) | async-done | bytes 4718608 | tf_op jit(solution)/shard_map/all_gather | solution.py:87
  102.8 2.8 fusion
  106.6 1.4 dynamic-slice_select_fusion
  108.1 87.4 %all-reduce.5.cloned.1.call-done = (f32[384,512]{0,1:T(8,128)}, f32[384,512]{0,1:T(8,128)}, f32[384,512]{0,1:T(8,128)}) async-done(((f32[384,512]{0,1:T(8,128)}, f32[384,512]{0,1:T(8,128)}, f32[384,512]{0,1:T(8,128)}), (f32[384,512]{0,1:T(8,128)}, f32[384,512]{0,1:T(8,128)}, f32[384,512]{0,1:T(8,128)})) %all-reduce.5.cloned.1.call-update) | async-done | bytes 2359312 | tf_op jit(solution)/shard_map/psum | solution.py:15
  195.5 3.6 fusion.3
  199.1 8.3 %all-to-all-start = ((f32[16,32,384]{2,1,0:T(8,128)}), f32[16,32,384]{2,1,0:T(8,128)}, u32[]{:S(2)}, u32[]{:S(2)}) async-start(f32[16,32,384]{2,1,0:T(8,128)} %fusion.3), calls=%async_computation | async-start | bytes 1572864 | tf_op jit(solution)/shard_map/all_to_all | solution.py:27
  207.8 22.4 %all-to-all-done = f32[16,32,384]{2,1,0:T(8,128)} async-done(((f32[16,32,384]{2,1,0:T(8,128)}), f32[16,32,384]{2,1,0:T(8,128)}, u32[]{:S(2)}, u32[]{:S(2)}) %all-to-all-start) | async-done | bytes 786464 | tf_op jit(solution)/shard_map/all_to_all | solution.py:27
  231.4 8.4 %all-reduce.7.cloned.1.call-done = (f32[384,512]{0,1:T(8,128)}, f32[384,512]{0,1:T(8,128)}, f32[384,512]{0,1:T(8,128)}) async-done(((f32[384,512]{0,1:T(8,128)}, f32[384,512]{0,1:T(8,128)}, f32[384,512]{0,1:T(8,128)}), (f32[384,512]{0,1:T(8,128)}, f32[384,512]{0,1:T(8,128)}, f32[384,512]{0,1:T(8,128)})) %all-reduce.7.cloned.1.call-update) | async-done | bytes 2359312 | tf_op jit(solution)/shard_map/psum | solution.py:15
  239.8 2.0 convolution_bitcast_fusion.3
  242.5 8.3 %all-to-all-start.5 = ((f32[32,1,512]{2,1,0:T(1,128)}), f32[32,1,512]{2,1,0:T(1,128)S(1)}, u32[]{:S(2)}, u32[]{:S(2)}) async-start(f32[32,1,512]{2,1,0:T(1,128)} %copy.9), calls=%async_computation.5 | async-start | bytes 131072 | tf_op jit(solution)/shard_map/all_to_all | solution.py:27
  250.8 2.0 convolution_bitcast_fusion.4
  253.4 6.2 %all-to-all-done.5 = f32[32,1,512]{2,1,0:T(1,128)S(1)} async-done(((f32[32,1,512]{2,1,0:T(1,128)}), f32[32,1,512]{2,1,0:T(1,128)S(1)}, u32[]{:S(2)}, u32[]{:S(2)}) %all-to-all-start.5) | async-done | bytes 65568 | tf_op jit(solution)/shard_map/all_to_all | solution.py:27
  259.6 3.9 all-to-all-start.3
  263.5 1.5 fusion.64
  265.1 7.3 %all-to-all-done.3 = f32[32,1,512]{2,1,0:T(1,128)S(1)} async-done(((f32[32,1,512]{2,1,0:T(1,128)}), f32[32,1,512]{2,1,0:T(1,128)S(1)}, u32[]{:S(2)}, u32[]{:S(2)}) %all-to-all-start.3) | async-done | bytes 65568 | tf_op jit(solution)/shard_map/all_to_all | solution.py:27
  273.0 3.9 all-to-all-start.6
  276.9 2.6 fusion.21
  279.5 6.2 %all-to-all-done.6 = f32[32,1,512]{2,1,0:T(1,128)S(1)} async-done(((f32[32,1,512]{2,1,0:T(1,128)}), f32[32,1,512]{2,1,0:T(1,128)S(1)}, u32[]{:S(2)}, u32[]{:S(2)}) %all-to-all-start.6) | async-done | bytes 65568 | tf_op jit(solution)/shard_map/all_to_all | solution.py:46
  286.4 3.9 all-to-all-start.4
  290.3 5.1 %convolution_add_fusion.1 = f32[512,384]{1,0:T(8,128)} fusion(f32[512,384]{1,0:T(8,128)} %fusion.21, f32[768,512]{0,1:T(8,128)} %copy-done.3, f32[768,384]{1,0:T(8,128)S(1)} %copy-done), kind=kOutput, calls=%fused_computation.7 | convolution fusion | flops 1812135936 | bytes 4325376 | tf_op jit(solution)/shard_map/dot_general | solution.py:65
  295.4 3.7 all-to-all-done.4
  299.1 12.6 %all-to-all-start.1 = ((f32[16,32,384]{2,1,0:T(8,128)}), f32[16,32,384]{2,1,0:T(8,128)}, u32[]{:S(2)}, u32[]{:S(2)}) async-start(f32[16,32,384]{2,1,0:T(8,128)} %bitcast.123), calls=%async_computation.1 | async-start | bytes 1572864 | tf_op jit(solution)/shard_map/all_to_all | solution.py:27
  312.8 2.2 convolution_add_fusion.3
  315.4 19.6 %all-to-all-done.1 = f32[16,32,384]{2,1,0:T(8,128)} async-done(((f32[16,32,384]{2,1,0:T(8,128)}), f32[16,32,384]{2,1,0:T(8,128)}, u32[]{:S(2)}, u32[]{:S(2)}) %all-to-all-start.1) | async-done | bytes 786464 | tf_op jit(solution)/shard_map/all_to_all | solution.py:27
  335.0 1.2 reduce_sum.80
  336.2 2.0 convolution_bitcast_fusion.2
  338.9 4.1 all-to-all-start.7
  343.0 2.0 convolution_bitcast_fusion.1
  345.7 6.2 %all-to-all-done.7 = f32[32,1,512]{2,1,0:T(1,128)S(1)} async-done(((f32[32,1,512]{2,1,0:T(1,128)}), f32[32,1,512]{2,1,0:T(1,128)S(1)}, u32[]{:S(2)}, u32[]{:S(2)}) %all-to-all-start.7) | async-done | bytes 65568 | tf_op jit(solution)/shard_map/all_to_all | solution.py:27
  352.5 3.9 all-to-all-start.9
  357.3 8.5 %all-to-all-done.9 = f32[32,1,512]{2,1,0:T(1,128)S(1)} async-done(((f32[32,1,512]{2,1,0:T(1,128)}), f32[32,1,512]{2,1,0:T(1,128)S(1)}, u32[]{:S(2)}, u32[]{:S(2)}) %all-to-all-start.9) | async-done | bytes 65568 | tf_op jit(solution)/shard_map/all_to_all | solution.py:27
  366.4 3.9 all-to-all-start.8
  370.3 2.6 fusion.19
  373.8 5.4 %all-to-all-done.8 = f32[32,1,512]{2,1,0:T(1,128)S(1)} async-done(((f32[32,1,512]{2,1,0:T(1,128)}), f32[32,1,512]{2,1,0:T(1,128)S(1)}, u32[]{:S(2)}, u32[]{:S(2)}) %all-to-all-start.8) | async-done | bytes 65568 | tf_op jit(solution)/shard_map/all_to_all | solution.py:46
  379.9 4.6 all-to-all-start.10
  384.4 5.1 %convolution_add_fusion = f32[512,384]{1,0:T(8,128)} fusion(f32[512,384]{1,0:T(8,128)} %fusion.19, f32[768,512]{0,1:T(8,128)} %copy-done.2, f32[768,384]{1,0:T(8,128)S(1)} %copy-done), kind=kOutput, calls=%fused_computation.6 | convolution fusion | flops 1812135936 | bytes 4325376 | tf_op jit(solution)/shard_map/dot_general | solution.py:65
  389.6 3.8 all-to-all-done.10
  393.4 7.4 %all-to-all-start.2 = ((f32[16,32,384]{2,1,0:T(8,128)}), f32[16,32,384]{2,1,0:T(8,128)}, u32[]{:S(2)}, u32[]{:S(2)}) async-start(f32[16,32,384]{2,1,0:T(8,128)} %bitcast.122), calls=%async_computation.2 | async-start | bytes 1572864 | tf_op jit(solution)/shard_map/all_to_all | solution.py:27
  400.9 1.7 convolution_add_fusion.5
  403.2 1.3 convolution_add_fusion.2
  406.8 17.4 %all-to-all-done.2 = f32[16,32,384]{2,1,0:T(8,128)} async-done(((f32[16,32,384]{2,1,0:T(8,128)}), f32[16,32,384]{2,1,0:T(8,128)}, u32[]{:S(2)}, u32[]{:S(2)}) %all-to-all-start.2) | async-done | bytes 786464 | tf_op jit(solution)/shard_map/all_to_all | solution.py:27
  425.3 2.0 convolution_bitcast_fusion
  428.0 4.6 all-to-all-start.11
  432.6 1.5 pad_maximum_fusion.1
  434.1 7.3 %all-to-all-done.11 = f32[32,1,512]{2,1,0:T(1,128)} async-done(((f32[32,1,512]{2,1,0:T(1,128)}), f32[32,1,512]{2,1,0:T(1,128)}, u32[]{:S(2)}, u32[]{:S(2)}) %all-to-all-start.11) | async-done | bytes 65568 | tf_op jit(solution)/shard_map/all_to_all | solution.py:27
  442.9 4.5 all-to-all-start.12
  449.0 7.4 %all-to-all-done.12 = f32[32,1,512]{2,1,0:T(1,128)} async-done(((f32[32,1,512]{2,1,0:T(1,128)}), f32[32,1,512]{2,1,0:T(1,128)}, u32[]{:S(2)}, u32[]{:S(2)}) %all-to-all-start.12) | async-done | bytes 65568 | tf_op jit(solution)/shard_map/all_to_all | solution.py:46
  456.4 1.7 fusion.5
  (70 shorter events, 24.6 us)
Async XLA Ops:
  7.2 188.4 %copy-start = (f32[768,384]{1,0:T(8,128)S(1)}, f32[768,384]{1,0:T(8,128)}, u32[]{:S(2)}) copy-start(f32[768,384]{1,0:T(8,128)} %param.5) | copy-start | bytes 3538948
  7.2 95.6 %all-gather.4.cloned.1.call-start = ((), (), s32[]{:S(2)}) async-start(), calls=%async_computation.13 | async-start | bytes 4866048 | tf_op jit(solution)/shard_map/all_gather | solution.py:87
  7.9 187.6 %all-reduce.5.cloned.1.call-start = ((), (), s32[]{:S(2)}) async-start(), calls=%async_computation.16 | async-start | bytes 4718592 | tf_op jit(solution)/shard_map/psum | solution.py:15
  105.6 2.4 copy-start.2
  105.6 2.4 copy-start.3
  108.0 131.8 %all-reduce.7.cloned.1.call-start = ((), (), s32[]{:S(2)}) async-start(), calls=%async_computation.17 | async-start | bytes 4718592 | tf_op jit(solution)/shard_map/psum | solution.py:15
  199.1 8.3 %copy-start.11 = (s32[3,96]{1,0:T(4,128)S(1)}, s32[3,96]{1,0:T(4,128)}, u32[]{:S(2)}) copy-start(s32[3,96]{1,0:T(4,128)} %param.6) | copy-start | bytes 3460
  199.1 31.1 %all-to-all-start = ((f32[16,32,384]{2,1,0:T(8,128)}), f32[16,32,384]{2,1,0:T(8,128)}, u32[]{:S(2)}, u32[]{:S(2)}) async-start(f32[16,32,384]{2,1,0:T(8,128)} %fusion.3), calls=%async_computation | async-start | bytes 1572864 | tf_op jit(solution)/shard_map/all_to_all | solution.py:27
  207.8 55.7 %copy-start.1 = (f32[2,512,512]{2,1,0:T(8,128)S(1)}, f32[2,512,512]{2,1,0:T(8,128)}, u32[]{:S(2)}) copy-start(f32[2,512,512]{2,1,0:T(8,128)} %param.8) | copy-start | bytes 6291460
  242.5 17.1 %all-to-all-start.5 = ((f32[32,1,512]{2,1,0:T(1,128)}), f32[32,1,512]{2,1,0:T(1,128)S(1)}, u32[]{:S(2)}, u32[]{:S(2)}) async-start(f32[32,1,512]{2,1,0:T(1,128)} %copy.9), calls=%async_computation.5 | async-start | bytes 131072 | tf_op jit(solution)/shard_map/all_to_all | solution.py:27
  259.6 12.7 %all-to-all-start.3 = ((f32[32,1,512]{2,1,0:T(1,128)}), f32[32,1,512]{2,1,0:T(1,128)S(1)}, u32[]{:S(2)}, u32[]{:S(2)}) async-start(f32[32,1,512]{2,1,0:T(1,128)} %copy.8), calls=%async_computation.3 | async-start | bytes 131072 | tf_op jit(solution)/shard_map/all_to_all | solution.py:27
  273.0 12.7 %all-to-all-start.6 = ((f32[32,1,512]{2,1,0:T(1,128)}), f32[32,1,512]{2,1,0:T(1,128)S(1)}, u32[]{:S(2)}, u32[]{:S(2)}) async-start(f32[32,1,512]{2,1,0:T(1,128)} %broadcast_in_dim.11), calls=%async_computation.6 | async-start | bytes 131072 | tf_op jit(solution)/shard_map/all_to_all | solution.py:46
  286.4 12.7 %all-to-all-start.4 = ((f32[32,1,512]{2,1,0:T(1,128)}), f32[32,1,512]{2,1,0:T(1,128)S(1)}, u32[]{:S(2)}, u32[]{:S(2)}) async-start(f32[32,1,512]{2,1,0:T(1,128)} %broadcast_in_dim.10), calls=%async_computation.4 | async-start | bytes 131072 | tf_op jit(solution)/shard_map/all_to_all | solution.py:46
  299.1 12.6 %copy-start.7 = (f32[32,1,512]{2,1,0:T(1,128)}, f32[32,1,512]{2,1,0:T(1,128)S(1)}, u32[]{:S(2)}) copy-start(f32[32,1,512]{2,1,0:T(1,128)S(1)} %all-to-all-done.4) | copy-start | bytes 196612
  299.1 35.9 %all-to-all-start.1 = ((f32[16,32,384]{2,1,0:T(8,128)}), f32[16,32,384]{2,1,0:T(8,128)}, u32[]{:S(2)}, u32[]{:S(2)}) async-start(f32[16,32,384]{2,1,0:T(8,128)} %bitcast.123), calls=%async_computation.1 | async-start | bytes 1572864 | tf_op jit(solution)/shard_map/all_to_all | solution.py:27
  311.7 89.1 %all-gather.6.cloned.1.call-start = ((), (), s32[]{:S(2)}) async-start(), calls=%async_computation.14 | async-start | bytes 1114112 | tf_op jit(solution)/shard_map/all_gather | solution.py:106
  338.9 13.0 %all-to-all-start.7 = ((f32[32,1,512]{2,1,0:T(1,128)}), f32[32,1,512]{2,1,0:T(1,128)S(1)}, u32[]{:S(2)}, u32[]{:S(2)}) async-start(f32[32,1,512]{2,1,0:T(1,128)} %copy.10), calls=%async_computation.7 | async-start | bytes 131072 | tf_op jit(solution)/shard_map/all_to_all | solution.py:27
  351.9 0.6 copy-start.9
  352.5 13.3 %all-to-all-start.9 = ((f32[32,1,512]{2,1,0:T(1,128)}), f32[32,1,512]{2,1,0:T(1,128)S(1)}, u32[]{:S(2)}, u32[]{:S(2)}) async-start(f32[32,1,512]{2,1,0:T(1,128)} %copy.11), calls=%async_computation.9 | async-start | bytes 131072 | tf_op jit(solution)/shard_map/all_to_all | solution.py:27
  365.8 0.7 copy-start.8
  366.4 12.7 %all-to-all-start.8 = ((f32[32,1,512]{2,1,0:T(1,128)}), f32[32,1,512]{2,1,0:T(1,128)S(1)}, u32[]{:S(2)}, u32[]{:S(2)}) async-start(f32[32,1,512]{2,1,0:T(1,128)} %broadcast_in_dim.12), calls=%async_computation.8 | async-start | bytes 131072 | tf_op jit(solution)/shard_map/all_to_all | solution.py:46
  379.9 13.5 %all-to-all-start.10 = ((f32[32,1,512]{2,1,0:T(1,128)}), f32[32,1,512]{2,1,0:T(1,128)}, u32[]{:S(2)}, u32[]{:S(2)}) async-start(f32[32,1,512]{2,1,0:T(1,128)} %broadcast_in_dim.13), calls=%async_computation.10 | async-start | bytes 131072 | tf_op jit(solution)/shard_map/all_to_all | solution.py:46
  393.4 30.7 %all-to-all-start.2 = ((f32[16,32,384]{2,1,0:T(8,128)}), f32[16,32,384]{2,1,0:T(8,128)}, u32[]{:S(2)}, u32[]{:S(2)}) async-start(f32[16,32,384]{2,1,0:T(8,128)} %bitcast.122), calls=%async_computation.2 | async-start | bytes 1572864 | tf_op jit(solution)/shard_map/all_to_all | solution.py:27
  400.8 55.6 %all-gather.8.cloned.1.call-start = ((), (), s32[]{:S(2)}) async-start(), calls=%async_computation.15 | async-start | bytes 1114112 | tf_op jit(solution)/shard_map/all_gather | solution.py:106
  402.6 0.6 copy-start.5
  404.6 42.9 %copy-start.4 = (f32[32,512]{1,0:T(8,128)S(1)}, f32[32,512]{1,0:T(8,128)}, u32[]{:S(2)}) copy-start(f32[32,512]{1,0:T(8,128)} %convolution_add_fusion.3) | copy-start | bytes 196612
  406.7 25.8 %copy-start.10 = (f32[384]{0:T(512)S(1)}, f32[384]{0:T(512)}, u32[]{:S(2)}) copy-start(f32[384]{0:T(512)} %convolution_reduce_fusion.3) | copy-start | bytes 4612
  427.3 30.9 %copy-start.6 = (f32[32,512]{1,0:T(8,128)S(1)}, f32[32,512]{1,0:T(8,128)}, u32[]{:S(2)}) copy-start(f32[32,512]{1,0:T(8,128)} %copy-done.5) | copy-start | bytes 196612
  428.0 13.4 %all-to-all-start.11 = ((f32[32,1,512]{2,1,0:T(1,128)}), f32[32,1,512]{2,1,0:T(1,128)}, u32[]{:S(2)}, u32[]{:S(2)}) async-start(f32[32,1,512]{2,1,0:T(1,128)} %copy.12), calls=%async_computation.11 | async-start | bytes 131072 | tf_op jit(solution)/shard_map/all_to_all | solution.py:27
  442.9 13.5 %all-to-all-start.12 = ((f32[32,1,512]{2,1,0:T(1,128)}), f32[32,1,512]{2,1,0:T(1,128)}, u32[]{:S(2)}, u32[]{:S(2)}) async-start(f32[32,1,512]{2,1,0:T(1,128)} %broadcast_in_dim.14), calls=%async_computation.12 | async-start | bytes 131072 | tf_op jit(solution)/shard_map/all_to_all | solution.py:46
Sparse Core Ops, SparseCore 0:
  11.2 91.5 all-gather.3
  108.1 87.3 all-reduce.4
  198.6 41.2 all-reduce.6
  315.2 39.2 all-gather.5
  404.7 38.7 all-gather.7
where the time goes:
time: 467 us; the launch traced here: 465 us
  waiting for transfers between devices  310 us (66%)
  starting transfers between devices  74.1 us (16%)
  matrix products  40.5 us (9%)
  other arithmetic  17.4 us (4%)
  between operations  14.1 us (3%)
  local copies, waits for them, and re-layouts  9.62 us (2%)
    psum x2, waiting for transfers between devices, broadcast_by_axis(): x = lax.psum(x, axis)  95.9 us
    all_to_all x8, waiting for transfers between devices, sent_and_summed(): pieces = lax.all_to_all(split_up(x, dim, length), axis, 0, 0, tiled=True)  94.9 us
    all_gather x1, waiting for transfers between devices, body(): fetched = lax.all_gather(factor_front, 'col', axis=2, tiled=True)  91.5 us
    all_to_all x8, starting transfers between devices, sent_and_summed(): pieces = lax.all_to_all(split_up(x, dim, length), axis, 0, 0, tiled=True)  53 us
    all_to_all x5, waiting for transfers between devices, from_everyone(): return lax.all_to_all(copies, axis, split_axis=0, concat_axis=0, tiled=True)  26.6 us
    dot_general x7, matrix products, contract_first(): lax.dot_general(former, latter, (((0,), (0,)), ((), ())), precision=HIGH,...  22.4 us
    all_to_all x5, starting transfers between devices, from_everyone(): return lax.all_to_all(copies, axis, split_axis=0, concat_axis=0, tiled=True)  20.7 us
    dot_general x7, matrix products, matmul(): jnp.dot(former, latter, precision=HIGH, preferred_element_type=jnp.float32)  13.3 us
  transfers between devices with their start and end apart: 18, of which 16 were waited for; matrix products, arithmetic and copies ran while one was open for 12% of the time, Pallas kernels for 0%

commit v1 on v0

--- a/solution.py
+++ b/solution.py
@@ -12,7 +12,7 @@
 def broadcast_by_axis(x, axes, root):
     x = jnp.where(lax.axis_index(axes) == root, x, jnp.zeros_like(x))
     for axis in axes:
-        x = lax.psum(x, axis)
+        x = jnp.sum(lax.all_gather(x, axis), axis=0)
     return x
 
 

time: 467 us -> 635 us (1.36); the launches traced: 465 us -> 625 us
  waiting for transfers between devices: 310 us -> 420 us
  other arithmetic: 17.4 us -> 38.5 us
  local copies, waits for them, and re-layouts: 9.62 us -> 30.6 us
  starting transfers between devices: 74.1 us -> 81 us
    all_gather x0 -> x6, waiting for transfers between devices: none -> 243 us  [broadcast_by_axis(): x = jnp.sum(lax.all_gather(x, axis), axis=0)]
    psum x2 -> x0, waiting for transfers between devices: 95.9 us -> none  [broadcast_by_axis(): x = lax.psum(x, axis)]
    all_to_all x8, waiting for transfers between devices: 94.9 us -> 59.6 us  [sent_and_summed(): pieces = lax.all_to_all(split_up(x, dim, length), axis, 0, 0, tiled=True)]
    reduce_sum x0 -> x6, other arithmetic: none -> 18.8 us  [broadcast_by_axis(): x = jnp.sum(lax.all_gather(x, axis), axis=0)]
    unnamed x24 -> x27, local copies, waits for them, and re-layouts: 1.3 us -> 14.3 us
    all_gather x0 -> x3, local copies, waits for them, and re-layouts: none -> 8.03 us  [broadcast_by_axis(): x = jnp.sum(lax.all_gather(x, axis), axis=0)]
  transfers between devices with their start and end apart: 18 -> 22, of which waited for: 16 -> 16; matrix products, arithmetic and copies ran while one was open for 12% -> 16% of each run, Pallas kernels for 0% -> 0%
where the time goes in v1:
time: 635 us; the launch traced here: 625 us
  waiting for transfers between devices  420 us (66%)
  starting transfers between devices  81 us (13%)
  matrix products  40.2 us (6%)
  other arithmetic  38.5 us (6%)
  local copies, waits for them, and re-layouts  30.6 us (5%)
  between operations  14.5 us (2%)
    all_gather x6, waiting for transfers between devices, broadcast_by_axis(): x = jnp.sum(lax.all_gather(x, axis), axis=0)  243 us
    all_gather x1, waiting for transfers between devices, body(): fetched = lax.all_gather(factor_front, 'col', axis=2, tiled=True)  91.5 us
    all_to_all x8, waiting for transfers between devices, sent_and_summed(): pieces = lax.all_to_all(split_up(x, dim, length), axis, 0, 0, tiled=True)  59.6 us
    all_to_all x8, starting transfers between devices, sent_and_summed(): pieces = lax.all_to_all(split_up(x, dim, length), axis, 0, 0, tiled=True)  59.1 us
    all_to_all x5, waiting for transfers between devices, from_everyone(): return lax.all_to_all(copies, axis, split_axis=0, concat_axis=0, tiled=True)  25.4 us
    dot_general x7, matrix products, contract_first(): lax.dot_general(former, latter, (((0,), (0,)), ((), ())), precision=HIGH,...  22.4 us
    all_to_all x5, starting transfers between devices, from_everyone(): return lax.all_to_all(copies, axis, split_axis=0, concat_axis=0, tiled=True)  21.1 us
    reduce_sum x6, other arithmetic, broadcast_by_axis(): x = jnp.sum(lax.all_gather(x, axis), axis=0)  18.8 us
  transfers between devices with their start and end apart: 22, of which 16 were waited for; matrix products, arithmetic and copies ran while one was open for 16% of the time, Pallas kernels for 0%

profile of v1, /device:TPU:1, one launch (start us, length us, event | category | flops | bytes accessed | tf_op | source)
XLA Modules:
  0.0 625.2 jit_solution(4041857294623762418)
XLA Ops:
  11.3 91.5 %all-gather.16.cloned.1.call-done = f32[3,768,512]{1,2,0:T(8,128)} async-done(((f32[3,768,16]{1,2,0:T(8,128)}), f32[3,768,512]{1,2,0:T(8,128)}) %all-gather.16.cloned.1.call-update) | async-done | bytes 4718608 | tf_op jit(solution)/shard_map/all_gather | solution.py:87
  102.8 4.0 fusion
  109.9 2.1 dynamic-slice_select_fusion
  112.1 75.1 %all-gather.22.cloned.1.call-done = f32[3072,512]{0,1:T(8,128)} async-done(((f32[384,512]{0,1:T(8,128)}), f32[3072,512]{0,1:T(8,128)}) %all-gather.22.cloned.1.call-update) | async-done | bytes 6291472 | tf_op jit(solution)/shard_map/all_gather | solution.py:15
  187.2 4.2 copy.23
  191.4 2.8 bitcast_reduce_fusion.2
  194.2 3.5 fusion.3
  197.7 4.9 all-to-all-start
  202.6 79.5 %all-gather.26.cloned.1.call-done = f32[3072,512]{0,1:T(8,128)} async-done(((f32[384,512]{0,1:T(8,128)}), f32[3072,512]{0,1:T(8,128)}) %all-gather.26.cloned.1.call-update) | async-done | bytes 6291472 | tf_op jit(solution)/shard_map/all_gather | solution.py:15
  282.2 4.2 copy.24
  286.3 2.8 bitcast_reduce_fusion.1
  290.7 69.4 %all-gather.30.cloned.1.call-done = f32[3072,512]{0,1:T(8,128)} async-done(((f32[384,512]{0,1:T(8,128)}), f32[3072,512]{0,1:T(8,128)}) %all-gather.30.cloned.1.call-update) | async-done | bytes 6291472 | tf_op jit(solution)/shard_map/all_gather | solution.py:15
  360.1 4.2 copy.25
  364.3 2.8 bitcast_reduce_fusion
  367.1 12.5 %all-gather.24.cloned.1.call-done = f32[768,512]{0,1:T(8,128)} async-done(((f32[384,512]{0,1:T(8,128)}), f32[768,512]{0,1:T(8,128)}) %all-gather.24.cloned.1.call-update) | async-done | bytes 1572880 | tf_op jit(solution)/shard_map/all_gather | solution.py:15
  379.6 2.1 reshape.217
  386.0 8.3 %all-to-all-start.3 = ((f32[32,1,512]{2,1,0:T(1,128)}), f32[32,1,512]{2,1,0:T(1,128)S(1)}, u32[]{:S(2)}, u32[]{:S(2)}) async-start(f32[32,1,512]{2,1,0:T(1,128)} %copy.13), calls=%async_computation.3 | async-start | bytes 131072 | tf_op jit(solution)/shard_map/all_to_all | solution.py:27
  394.3 6.6 %all-gather.28.cloned.1.call-done = f32[768,512]{0,1:T(8,128)} async-done(((f32[384,512]{0,1:T(8,128)}), f32[768,512]{0,1:T(8,128)}) %all-gather.28.cloned.1.call-update) | async-done | bytes 1572880 | tf_op jit(solution)/shard_map/all_gather | solution.py:15
  400.8 2.9 reshape.219
  403.8 4.3 reduce_sum.142
  410.7 8.3 %all-to-all-start.5 = ((f32[32,1,512]{2,1,0:T(1,128)}), f32[32,1,512]{2,1,0:T(1,128)S(1)}, u32[]{:S(2)}, u32[]{:S(2)}) async-start(f32[32,1,512]{2,1,0:T(1,128)} %copy.14), calls=%async_computation.5 | async-start | bytes 131072 | tf_op jit(solution)/shard_map/all_to_all | solution.py:27
  420.6 7.3 %all-to-all-done.5 = f32[32,1,512]{2,1,0:T(1,128)S(1)} async-done(((f32[32,1,512]{2,1,0:T(1,128)}), f32[32,1,512]{2,1,0:T(1,128)S(1)}, u32[]{:S(2)}, u32[]{:S(2)}) %all-to-all-start.5) | async-done | bytes 65568 | tf_op jit(solution)/shard_map/all_to_all | solution.py:27
  428.5 4.0 all-to-all-start.4
  432.6 2.6 fusion.21
  436.1 5.4 all-to-all-done.4
  442.1 3.9 all-to-all-start.6
  446.0 5.1 convolution_add_fusion.1
  451.1 3.7 all-to-all-done.6
  454.8 11.4 %all-to-all-start.1 = ((f32[16,32,384]{2,1,0:T(8,128)}), f32[16,32,384]{2,1,0:T(8,128)}, u32[]{:S(2)}, u32[]{:S(2)}) async-start(f32[16,32,384]{2,1,0:T(8,128)} %bitcast.147), calls=%async_computation.1 | async-start | bytes 1572864 | tf_op jit(solution)/shard_map/all_to_all | solution.py:27
  468.9 20.7 %all-to-all-done.1 = f32[16,32,384]{2,1,0:T(8,128)} async-done(((f32[16,32,384]{2,1,0:T(8,128)}), f32[16,32,384]{2,1,0:T(8,128)}, u32[]{:S(2)}, u32[]{:S(2)}) %all-to-all-start.1) | async-done | bytes 786464 | tf_op jit(solution)/shard_map/all_to_all | solution.py:27
  493.4 4.1 all-to-all-start.9
  497.6 3.0 reshape.221
  500.5 4.2 reduce_sum.145
  507.4 9.4 %all-to-all-start.7 = ((f32[32,1,512]{2,1,0:T(1,128)}), f32[32,1,512]{2,1,0:T(1,128)}, u32[]{:S(2)}, u32[]{:S(2)}) async-start(f32[32,1,512]{2,1,0:T(1,128)} %copy.15), calls=%async_computation.7 | async-start | bytes 131072 | tf_op jit(solution)/shard_map/all_to_all | solution.py:27
  516.8 8.9 %all-to-all-done.7 = f32[32,1,512]{2,1,0:T(1,128)} async-done(((f32[32,1,512]{2,1,0:T(1,128)}), f32[32,1,512]{2,1,0:T(1,128)}, u32[]{:S(2)}, u32[]{:S(2)}) %all-to-all-start.7) | async-done | bytes 65568 | tf_op jit(solution)/shard_map/all_to_all | solution.py:27
  526.4 3.9 all-to-all-start.10
  530.2 2.6 fusion.19
  533.7 5.4 all-to-all-done.10
  539.8 4.8 all-to-all-start.8
  544.6 5.2 convolution_add_fusion
  549.7 3.7 all-to-all-done.8
  553.4 7.4 %all-to-all-start.2 = ((f32[16,32,384]{2,1,0:T(8,128)}), f32[16,32,384]{2,1,0:T(8,128)}, u32[]{:S(2)}, u32[]{:S(2)}) async-start(f32[16,32,384]{2,1,0:T(8,128)} %bitcast.146), calls=%async_computation.2 | async-start | bytes 1572864 | tf_op jit(solution)/shard_map/all_to_all | solution.py:27
  563.2 2.2 convolution_add_fusion.2
  567.5 15.4 %all-to-all-done.2 = f32[16,32,384]{2,1,0:T(8,128)} async-done(((f32[16,32,384]{2,1,0:T(8,128)}), f32[16,32,384]{2,1,0:T(8,128)}, u32[]{:S(2)}, u32[]{:S(2)}) %all-to-all-start.2) | async-done | bytes 786464 | tf_op jit(solution)/shard_map/all_to_all | solution.py:27
  586.8 5.4 all-to-all-start.11
  593.7 7.3 %all-to-all-done.11 = f32[32,1,512]{2,1,0:T(1,128)} async-done(((f32[32,1,512]{2,1,0:T(1,128)}), f32[32,1,512]{2,1,0:T(1,128)}, u32[]{:S(2)}, u32[]{:S(2)}) %all-to-all-start.11) | async-done | bytes 65568 | tf_op jit(solution)/shard_map/all_to_all | solution.py:27
  602.6 4.6 all-to-all-start.12
  608.7 7.3 %all-to-all-done.12 = f32[32,1,512]{2,1,0:T(1,128)} async-done(((f32[32,1,512]{2,1,0:T(1,128)}), f32[32,1,512]{2,1,0:T(1,128)}, u32[]{:S(2)}, u32[]{:S(2)}) %all-to-all-start.12) | async-done | bytes 65568 | tf_op jit(solution)/shard_map/all_to_all | solution.py:46
  (95 shorter events, 46.3 us)
Async XLA Ops:
  7.2 187.0 %copy-start = (f32[768,384]{1,0:T(8,128)S(1)}, f32[768,384]{1,0:T(8,128)}, u32[]{:S(2)}) copy-start(f32[768,384]{1,0:T(8,128)} %param.5) | copy-start | bytes 3538948
  7.2 95.6 %all-gather.16.cloned.1.call-start = ((), (), s32[]{:S(2)}) async-start(), calls=%async_computation.13 | async-start | bytes 4866048 | tf_op jit(solution)/shard_map/all_gather | solution.py:87
  7.9 179.3 %all-gather.22.cloned.1.call-start = ((), (), s32[]{:S(2)}) async-start(), calls=%async_computation.16 | async-start | bytes 7077888 | tf_op jit(solution)/shard_map/all_gather | solution.py:15
  106.7 1.1 copy-start.2
  108.8 173.3 %all-gather.26.cloned.1.call-start = ((), (), s32[]{:S(2)}) async-start(), calls=%async_computation.18 | async-start | bytes 7077888 | tf_op jit(solution)/shard_map/all_gather | solution.py:15
  109.9 250.2 %all-gather.30.cloned.1.call-start = ((), (), s32[]{:S(2)}) async-start(), calls=%async_computation.20 | async-start | bytes 7077888 | tf_op jit(solution)/shard_map/all_gather | solution.py:15
  112.0 267.5 %all-gather.24.cloned.1.call-start = ((), (), s32[]{:S(2)}) async-start(), calls=%async_computation.17 | async-start | bytes 2359296 | tf_op jit(solution)/shard_map/all_gather | solution.py:15
  197.7 92.3 %all-to-all-start = ((f32[16,32,384]{2,1,0:T(8,128)}), f32[16,32,384]{2,1,0:T(8,128)S(1)}, u32[]{:S(2)}, u32[]{:S(2)}) async-start(f32[16,32,384]{2,1,0:T(8,128)} %fusion.3), calls=%async_computation | async-start | bytes 1572864 | tf_op jit(solution)/shard_map/all_to_all | solution.py:27
  202.6 198.2 %all-gather.28.cloned.1.call-start = ((), (), s32[]{:S(2)}) async-start(), calls=%async_computation.19 | async-start | bytes 2359296 | tf_op jit(solution)/shard_map/all_gather | solution.py:15
  286.3 3.4 copy-start.11
  289.2 208.4 %all-gather.32.cloned.1.call-start = ((), (), s32[]{:S(2)}) async-start(), calls=%async_computation.21 | async-start | bytes 2359296 | tf_op jit(solution)/shard_map/all_gather | solution.py:15
  383.6 17.2 %copy-start.3 = (f32[384,512]{0,1:T(8,128)}, f32[384,512]{0,1:T(8,128)S(1)}, u32[]{:S(2)}) copy-start(f32[384,512]{0,1:T(8,128)S(1)} %reduce_sum.139) | copy-start | bytes 2359300
  386.0 24.7 %all-to-all-start.3 = ((f32[32,1,512]{2,1,0:T(1,128)}), f32[32,1,512]{2,1,0:T(1,128)S(1)}, u32[]{:S(2)}, u32[]{:S(2)}) async-start(f32[32,1,512]{2,1,0:T(1,128)} %copy.13), calls=%async_computation.3 | async-start | bytes 131072 | tf_op jit(solution)/shard_map/all_to_all | solution.py:27
  403.8 4.3 copy-start.4
  403.8 15.3 %copy-start.1 = (f32[2,512,512]{2,1,0:T(8,128)S(1)}, f32[2,512,512]{2,1,0:T(8,128)}, u32[]{:S(2)}) copy-start(f32[2,512,512]{2,1,0:T(8,128)} %param.8) | copy-start | bytes 6291460
  410.7 17.1 %all-to-all-start.5 = ((f32[32,1,512]{2,1,0:T(1,128)}), f32[32,1,512]{2,1,0:T(1,128)S(1)}, u32[]{:S(2)}, u32[]{:S(2)}) async-start(f32[32,1,512]{2,1,0:T(1,128)} %copy.14), calls=%async_computation.5 | async-start | bytes 131072 | tf_op jit(solution)/shard_map/all_to_all | solution.py:27
  427.9 0.7 copy-start.9
  428.5 12.9 %all-to-all-start.4 = ((f32[32,1,512]{2,1,0:T(1,128)}), f32[32,1,512]{2,1,0:T(1,128)S(1)}, u32[]{:S(2)}, u32[]{:S(2)}) async-start(f32[32,1,512]{2,1,0:T(1,128)} %broadcast_in_dim.10), calls=%async_computation.4 | async-start | bytes 131072 | tf_op jit(solution)/shard_map/all_to_all | solution.py:46
  442.1 12.7 %all-to-all-start.6 = ((f32[32,1,512]{2,1,0:T(1,128)}), f32[32,1,512]{2,1,0:T(1,128)S(1)}, u32[]{:S(2)}, u32[]{:S(2)}) async-start(f32[32,1,512]{2,1,0:T(1,128)} %broadcast_in_dim.11), calls=%async_computation.6 | async-start | bytes 131072 | tf_op jit(solution)/shard_map/all_to_all | solution.py:46
  454.8 11.4 %copy-start.8 = (f32[32,1,512]{2,1,0:T(1,128)}, f32[32,1,512]{2,1,0:T(1,128)S(1)}, u32[]{:S(2)}) copy-start(f32[32,1,512]{2,1,0:T(1,128)S(1)} %all-to-all-done.6) | copy-start | bytes 196612
  454.8 34.7 %all-to-all-start.1 = ((f32[16,32,384]{2,1,0:T(8,128)}), f32[16,32,384]{2,1,0:T(8,128)}, u32[]{:S(2)}, u32[]{:S(2)}) async-start(f32[16,32,384]{2,1,0:T(8,128)} %bitcast.147), calls=%async_computation.1 | async-start | bytes 1572864 | tf_op jit(solution)/shard_map/all_to_all | solution.py:27
  466.3 94.6 %all-gather.18.cloned.1.call-start = ((), (), s32[]{:S(2)}) async-start(), calls=%async_computation.14 | async-start | bytes 1114112 | tf_op jit(solution)/shard_map/all_gather | solution.py:106
  493.4 14.0 %all-to-all-start.9 = ((f32[32,1,512]{2,1,0:T(1,128)}), f32[32,1,512]{2,1,0:T(1,128)S(1)}, u32[]{:S(2)}, u32[]{:S(2)}) async-start(f32[32,1,512]{2,1,0:T(1,128)} %copy.16), calls=%async_computation.9 | async-start | bytes 131072 | tf_op jit(solution)/shard_map/all_to_all | solution.py:27
  507.4 18.3 %all-to-all-start.7 = ((f32[32,1,512]{2,1,0:T(1,128)}), f32[32,1,512]{2,1,0:T(1,128)}, u32[]{:S(2)}, u32[]{:S(2)}) async-start(f32[32,1,512]{2,1,0:T(1,128)} %copy.15), calls=%async_computation.7 | async-start | bytes 131072 | tf_op jit(solution)/shard_map/all_to_all | solution.py:27
  526.4 12.7 %all-to-all-start.10 = ((f32[32,1,512]{2,1,0:T(1,128)}), f32[32,1,512]{2,1,0:T(1,128)S(1)}, u32[]{:S(2)}, u32[]{:S(2)}) async-start(f32[32,1,512]{2,1,0:T(1,128)} %broadcast_in_dim.13), calls=%async_computation.10 | async-start | bytes 131072 | tf_op jit(solution)/shard_map/all_to_all | solution.py:46
  539.8 13.6 %all-to-all-start.8 = ((f32[32,1,512]{2,1,0:T(1,128)}), f32[32,1,512]{2,1,0:T(1,128)}, u32[]{:S(2)}, u32[]{:S(2)}) async-start(f32[32,1,512]{2,1,0:T(1,128)} %broadcast_in_dim.12), calls=%async_computation.8 | async-start | bytes 131072 | tf_op jit(solution)/shard_map/all_to_all | solution.py:46
  553.4 29.6 %all-to-all-start.2 = ((f32[16,32,384]{2,1,0:T(8,128)}), f32[16,32,384]{2,1,0:T(8,128)}, u32[]{:S(2)}, u32[]{:S(2)}) async-start(f32[16,32,384]{2,1,0:T(8,128)} %bitcast.146), calls=%async_computation.2 | async-start | bytes 1572864 | tf_op jit(solution)/shard_map/all_to_all | solution.py:27
  560.8 55.2 %all-gather.20.cloned.1.call-start = ((), (), s32[]{:S(2)}) async-start(), calls=%async_computation.15 | async-start | bytes 1114112 | tf_op jit(solution)/shard_map/all_gather | solution.py:106
  562.6 0.6 copy-start.6
  565.4 41.8 %copy-start.5 = (f32[32,512]{1,0:T(8,128)S(1)}, f32[32,512]{1,0:T(8,128)}, u32[]{:S(2)}) copy-start(f32[32,512]{1,0:T(8,128)} %convolution_add_fusion.3) | copy-start | bytes 196612
  567.5 24.7 %copy-start.10 = (f32[384]{0:T(512)S(1)}, f32[384]{0:T(512)}, u32[]{:S(2)}) copy-start(f32[384]{0:T(512)} %convolution_reduce_fusion.3) | copy-start | bytes 4612
  586.1 31.6 %copy-start.7 = (f32[32,512]{1,0:T(8,128)S(1)}, f32[32,512]{1,0:T(8,128)}, u32[]{:S(2)}) copy-start(f32[32,512]{1,0:T(8,128)} %copy-done.6) | copy-start | bytes 196612
  586.8 14.2 %all-to-all-start.11 = ((f32[32,1,512]{2,1,0:T(1,128)}), f32[32,1,512]{2,1,0:T(1,128)}, u32[]{:S(2)}, u32[]{:S(2)}) async-start(f32[32,1,512]{2,1,0:T(1,128)} %copy.17), calls=%async_computation.11 | async-start | bytes 131072 | tf_op jit(solution)/shard_map/all_to_all | solution.py:27
  602.6 13.4 %all-to-all-start.12 = ((f32[32,1,512]{2,1,0:T(1,128)}), f32[32,1,512]{2,1,0:T(1,128)}, u32[]{:S(2)}, u32[]{:S(2)}) async-start(f32[32,1,512]{2,1,0:T(1,128)} %broadcast_in_dim.14), calls=%async_computation.12 | async-start | bytes 131072 | tf_op jit(solution)/shard_map/all_to_all | solution.py:46
Sparse Core Ops, SparseCore 0:
  11.2 91.5 all-gather.15
  109.0 78.1 all-gather.21
  189.3 92.8 all-gather.25
  284.1 75.9 all-gather.29
  362.1 17.4 all-gather.23
  381.5 19.2 all-gather.27
  402.9 19.2 all-gather.31
  469.8 39.2 all-gather.17
  565.5 38.3 all-gather.19
